TPU v7x, 512 devices: a whole 4x4x16 slice. The times are simulated.
512 devices in a mesh: basis: 32 (over z_hi, x, core), query: 16 (over z_lo, y).
Axes of the slice: x: 4, y: 4, z: 16 (z_hi: 4, z_lo: 4; z = z_hi * 4 + z_lo), core: 2. Of those that a mesh axis runs over, the one named last changes fastest.
Arguments:
- train_inputs: bfloat16 [256, 8192], P(None, 'basis'), may hold values from -6 to 6
- train_grads: bfloat16 [256, 8192], P(None, 'query'), may hold values from -0.375 to 0.375
- example_ids: int32 [256], replicated, may hold values from 0 to 3, never falling along the last dimension, each value on 1 to 128 neighbouring positions
- task_ids: int32 [48, 1], replicated, may hold values from 0 to 15
- basis_in: bfloat16 [8192, 8192], P('basis', 'query'), may hold values from -0.0625 to 0.0625
- basis_out: bfloat16 [8192, 8192], P('query', 'basis'), may hold values from -0.0625 to 0.0625
- eigenvalues: float32 [8192, 8192], P('basis', 'query'), may hold values from 0.2 to 5
- query_in: bfloat16 [8192, 1536], P('basis'), may hold values from -0.0625 to 0.0625
- query_out: bfloat16 [8192, 1536], P('query'), may hold values from -0.0625 to 0.0625
Outputs:
- precond_total: bfloat16 [8192, 8192], P('basis', 'query')
- influence: float32 [4, 48], replicated
- task_influence: float32 [4, 16], replicated
Inputs may be any that keep to these rules, and one draw needn't show every extreme that they name: `example_ids`: example ids never fall along the rows; each example has 1 to 128 rows. `task_ids`: each task has one query or more.
All inputs are finite; a program needn't handle non-finite values.
Results may differ from a plain program's by a relative error of at most 0.0013.
Values sent between devices are 32-bit elements; how exact they have to be, the bound alone decides.
A program may use at most 64 MiB of HBM per device.

v0:
```python
import jax
import jax.numpy as jnp
from jax import lax
from jax.sharding import PartitionSpec as P

EXAMPLES = 4
QUERIES = 48
TASKS = 16
RANK = 32


DAMPING = 0.05


def contract_rows(left_side, right_side):
    return lax.dot_general(
        left_side, right_side, (((0,), (0,)), ((), ())), preferred_element_type=jnp.float32
    )


def contract_exact(left_side, right_side):
    return lax.dot_general(
        left_side,
        right_side,
        (((0,), (0,)), ((), ())),
        precision=lax.Precision.HIGHEST,
        preferred_element_type=jnp.float32,
    )


def shards(
    train_inputs,
    train_grads,
    example_ids,
    task_ids,
    basis_in,
    basis_out,
    eigenvalues,
    query_in,
    query_out,
):
    factor_out = contract_rows(basis_out, query_out)
    factor_in = contract_rows(basis_in, query_in)
    grad_term = jnp.dot(train_grads, basis_out, preferred_element_type=jnp.float32)
    input_term = jnp.dot(train_inputs, basis_in, preferred_element_type=jnp.float32)
    rot_grads, rot_query_out = lax.psum((grad_term, factor_out), "query")
    rot_inputs, rot_query_in = lax.psum((input_term, factor_in), "basis")
    denominator = eigenvalues + DAMPING
    running_sum = jnp.zeros(eigenvalues.shape, jnp.float32)
    partials = []
    for example in range(EXAMPLES):
        selected = jnp.where(
            (example_ids == example)[:, None], rot_grads, jnp.zeros_like(rot_grads)
        )
        scaled = contract_exact(selected, rot_inputs) / denominator
        running_sum = running_sum + scaled
        weighted = jnp.dot(
            scaled,
            rot_query_in,
            precision=lax.Precision.HIGHEST,
            preferred_element_type=jnp.float32,
        )
        partials.append(jnp.sum(weighted * rot_query_out, axis=0))
    partial_value = jnp.stack(partials).reshape(EXAMPLES, QUERIES, RANK).sum(axis=2)
    influence = lax.psum(partial_value, ("basis", "query"))
    task_table = (task_ids == jnp.arange(TASKS, dtype=jnp.int32)[None, :]).astype(jnp.float32)
    counts = jnp.sum(task_table, axis=0)
    task_influence = (
        jnp.dot(influence, task_table, precision=lax.Precision.HIGHEST) / counts[None, :]
    )
    return (running_sum.astype(jnp.bfloat16), influence, task_influence)


def solution(mesh):
    in_specs = (
        P(None, "basis"),
        P(None, "query"),
        P(),
        P(),
        P("basis", "query"),
        P("query", "basis"),
        P("basis", "query"),
        P("basis", None),
        P("query", None),
    )
    out_specs = (P("basis", "query"), P(), P())
    return jax.shard_map(shards, mesh=mesh, in_specs=in_specs, out_specs=out_specs, check_vma=False)
```

profile of v0, /device:TPU:1, one launch (start us, length us, event | category | flops | bytes accessed | tf_op | source)
XLA Modules:
  0.0 697.6 jit_solution(4493430370739674458)
XLA Ops:
  7.2 0.0 copy-start
  7.2 0.0 copy-start.4
  7.2 0.0 copy-start.8
  7.2 0.0 all-reduce.7.cloned.1.call-start
  7.2 1.3 copy-done
  8.6 2.8 fusion.24
  11.4 0.0 copy-done.4
  11.4 0.0 copy-done.8
  11.4 0.0 copy-start.3
  11.4 0.0 copy-start.10
  11.4 0.9 fusion.21
  12.3 0.0 copy-start.5
  12.3 0.0 all-reduce.7.cloned.1.call-update
  12.3 0.0 all-reduce.5.cloned.1.call-start
  12.4 0.0 copy-done.3
  12.4 0.0 copy-done.10
  12.4 1.0 fusion.22
  13.4 0.0 copy-done.5
  13.4 2.3 fusion.23
  15.7 0.0 copy-start.13
  15.7 0.0 all-reduce.5.cloned.1.call-update
  15.8 0.6 copy-done.13
  16.4 0.1 convert_reduce_fusion
  16.5 0.0 copy-done.12
  16.5 168.3 %all-reduce.7.cloned.1.call-done = (f32[256,256]{1,0:T(8,128)}, f32[256,1536]{1,0:T(8,128)}) async-done(((f32[256,256]{1,0:T(8,128)}, f32[256,1536]{1,0:T(8,128)}), (f32[256,256]{1,0:T(8,128)}, f32[256,1536]{1,0:T(8,128)})) %all-reduce.7.cloned.1.call-update) | async-done | bytes 1835024 | tf_op jit(solution)/shard_map/psum | solution.py:46
  184.9 380.5 %all-reduce.5.cloned.1.call-done = (f32[256,512]{1,0:T(8,128)}, f32[512,1536]{1,0:T(8,128)}) async-done(((f32[256,512]{1,0:T(8,128)}, f32[512,1536]{1,0:T(8,128)}), (f32[256,512]{1,0:T(8,128)}, f32[512,1536]{1,0:T(8,128)})) %all-reduce.5.cloned.1.call-update) | async-done | bytes 3670032 | tf_op jit(solution)/shard_map/psum | solution.py:47
  565.3 0.0 copy-done.6
  565.3 2.0 convolution_divide_fusion.1
  567.3 0.0 copy-done.9
  567.3 0.0 copy-done.7
  567.3 0.0 copy-start.1
  567.4 0.7 convolution_divide_fusion.2
  568.1 0.7 convolution_divide_fusion.3
  568.8 0.0 copy-done.2
  568.8 0.4 copy-done.1
  569.2 2.9 fusion
  572.1 2.9 fusion.1
  575.0 2.9 fusion.2
  577.9 1.5 add_convert_fusion
  579.4 3.1 fusion.3
  582.4 0.1 stack.18
  582.5 0.1 stack.15
  582.6 0.1 stack.16
  582.7 0.1 stack.17
  582.7 0.1 maximum_reduce_fusion
  582.8 107.2 %psum.39 = f32[4,48]{1,0:T(4,128)S(1)} all-reduce(f32[4,48]{1,0:T(4,128)S(1)} %maximum_reduce_fusion), channel_id=1, replica_groups=mesh['basis'=32,'query'=16] {'basis','query'}, use_global_device_ids=true, to_apply=%region_9.10 | all-reduce | flops 192 | bytes 1536 | tf_op jit(solution)/shard_map/psum | solution.py:65
  690.0 0.7 convolution_divide_fusion.4
  690.7 0.0 copy-done.11
  (7 shorter events, 0.0 us)
Async XLA Ops:
  7.2 1.4 copy-start
  7.2 4.2 copy-start.4
  7.2 4.2 copy-start.8
  7.2 177.6 %all-reduce.7.cloned.1.call-start = ((), (), s32[]{:S(2)}) async-start(), calls=%async_computation.1 | async-start | bytes 3670016 | tf_op jit(solution)/shard_map/psum | solution.py:46
  11.4 1.0 copy-start.3
  11.4 1.0 copy-start.10
  12.3 1.1 copy-start.5
  12.3 553.0 %all-reduce.5.cloned.1.call-start = ((), (), s32[]{:S(2)}) async-start(), calls=%async_computation | async-start | bytes 7340032 | tf_op jit(solution)/shard_map/psum | solution.py:47
  15.7 0.7 copy-start.13
  15.7 0.8 copy-start.12
  15.7 549.6 %copy-start.6 = (f32[256,512]{1,0:T(8,128)S(1)}, f32[256,512]{1,0:T(8,128)}, u32[]{:S(2)}) copy-start(f32[256,512]{1,0:T(8,128)} %param.15) | copy-start | bytes 1572868
  184.8 382.5 %copy-start.9 = (f32[256,256]{1,0:T(8,128)S(1)}, f32[256,256]{1,0:T(8,128)}, u32[]{:S(2)}) copy-start(f32[256,256]{1,0:T(8,128)} %get-tuple-element.5) | copy-start | bytes 786436
  565.3 2.0 copy-start.7
  565.3 3.5 copy-start.2
  567.3 1.9 copy-start.1
  690.0 0.7 copy-start.11
Sparse Core Ops, SparseCore 0:
  12.4 172.3 all-reduce.6
  188.1 377.1 all-reduce.4
where the time goes:
time: 698 us
  waiting for transfers between devices  549 us (79%)
  blocking collectives  107 us (15%)
  matrix products  24.3 us (3%)
  between operations  14.2 us (2%)
    psum x1, waiting for transfers between devices, shards(): rot_inputs, rot_query_in = lax.psum((input_term, factor_in), 'basis')  380 us
    psum x1, waiting for transfers between devices, shards(): rot_grads, rot_query_out = lax.psum((grad_term, factor_out), 'query')  168 us
    psum x1, blocking collectives, shards(): influence = lax.psum(partial_value, ('basis', 'query'))  107 us
  transfers between devices with their start and end apart: 2, of which 2 were waited for; matrix products, arithmetic and copies ran while one was open for 0% of the time, Pallas kernels for 0%

commit v1 on v0

v1 whole, which is shorter than its diff:
```python
import functools

import jax
import jax.numpy as jnp
from jax import lax
from jax.experimental import pallas as pl
from jax.experimental.pallas import tpu as pltpu
from jax.sharding import PartitionSpec as P

EXAMPLES = 4
QUERIES = 48
TASKS = 16
RANK = 32
DAMPING = 0.05
TOKENS = 256
QC = QUERIES * RANK
JB = 512
IB = 256
LANES = 128

WIDTHS = (256, 512, 512, 512)
STARTS = tuple(sum(WIDTHS[:s]) for s in range(len(WIDTHS)))
STAGES = len(WIDTHS)
TOTAL = sum(WIDTHS)
MESH = pl.DeviceIdType.MESH
COPIES = 160


def dot(a, b, contract=((1,), (0,))):
    return lax.dot_general(a, b, (contract, ((), ())), preferred_element_type=jnp.float32)


def split(value):
    high = value.astype(jnp.bfloat16)
    return high, (value - high.astype(jnp.float32)).astype(jnp.bfloat16)


def select_dot(value, table):
    high, rest = split(value)
    mid = (value - high.astype(jnp.float32) - rest.astype(jnp.float32)).astype(jnp.bfloat16)
    return dot(high, table) + dot(rest, table) + dot(mid, table)


def kernel(
    h_tin, h_tgr, h_eid, h_tid, h_bin, h_bout, h_eig, h_qin, h_qout,
    o_total, o_inf, o_task,
    tin, tgr, eid, tid, b_in, b_out, eig, qin, qout,
    bt_in, bt_out, inv,
    pb, fb, ls, lx, lz, lw, cz, pq, fq, ly, le, li,
    s_hi, s_lo, part, ar_c, ar_x, ar_y, ar_l, ar_h,
    send_sem, recv_sem, load_sem,
):
    basis, query = lax.axis_index("basis"), lax.axis_index("query")
    zh, x, core = basis // 8, (basis // 2) % 4, basis % 2
    zl, y = query // 4, query % 4

    def dev(zh=zh, x=x, core=core, zl=zl, y=y):
        return (zh * 8 + x * 2 + core, zl * 4 + y)

    sibling = dev(core=1 - core)
    xs = [None] + [dev(x=(x + d) % 4) for d in (1, 2, 3)]
    ys = [None] + [dev(y=(y + d) % 4) for d in (1, 2, 3)]
    zhs = [None] + [dev(zh=(zh + d) % 4) for d in (1, 2, 3)]
    zls = [None] + [dev(zl=(zl + d) % 4) for d in (1, 2, 3)]

    loads = []
    for n, (src, dst) in enumerate((
        (h_bin, b_in), (h_tin, tin), (h_bout, b_out), (h_tgr, tgr), (h_qin, qin),
        (h_qout, qout), (h_eig, eig), (h_eid, eid), (h_tid, tid),
    )):
        load = pltpu.make_async_copy(src, dst, load_sem.at[n])
        load.start()
        loads.append(load)

    barrier = pltpu.get_barrier_semaphore()
    peers = [sibling] + xs[1:] + ys[1:] + zhs[1:] + zls[1:]
    for peer in peers:
        pl.semaphore_signal(barrier, inc=1, device_id=peer, device_id_type=MESH)

    made = [0]

    def copy(src, dst, target):
        n = made[0]
        made[0] += 1
        return pltpu.make_async_remote_copy(
            src_ref=src, dst_ref=dst, send_sem=send_sem.at[n], recv_sem=recv_sem.at[n],
            device_id=target, device_id_type=MESH,
        )

    unsent = []
    tick = [0]

    def send(src, dst, target):
        one = copy(src, dst, target)
        one.start()
        unsent.append((tick[0], one.wait_send))
        return one

    def drain(before):
        while unsent and unsent[0][0] < before:
            unsent.pop(0)[1]()

    def rows(ref, start, size):
        return ref.at[pl.ds(pl.multiple_of(start, 8), size)]

    def get(ref, start, size):
        return ref[pl.ds(pl.multiple_of(start, 8), size), :]

    def put(ref, start, size, value):
        ref[pl.ds(pl.multiple_of(start, 8), size), :] = value

    def basis_stage(s):
        width = WIDTHS[s]
        base = STARTS[s] * 4
        half = width * 2
        xr, zr = half // 4, half // 16
        za = zr // 2
        own = base + core * half
        mine = own + x * xr

        if s == 0:
            loads[0].wait()
            bt_in[...] = b_in[...].T
            loads[1].wait()
            value = dot(bt_in[...], tin[...], ((1,), (1,)))
        else:
            if s == 1:
                loads[4].wait()
            c = STARTS[s] - TOKENS
            value = dot(bt_in[...], qin[:, c:c + width])
        for tile in range(width // LANES):
            pb[base + tile * JB:base + (tile + 1) * JB, :] = value[:, tile * LANES:(tile + 1) * LANES]
        if s == 0:
            pl.semaphore_wait(barrier, len(peers))
        landing = ls.at[pl.ds(base // 2, half)]
        pair = send(rows(pb, base + (1 - core) * half, half), landing, sibling)
        yield

        pair.wait_recv()
        put(pb, own, half, get(pb, own, half) + ls[base // 2:base // 2 + half, :])
        lxo = base // 8
        sent = [
            send(rows(pb, own + ((x + d) % 4) * xr, xr), lx.at[d - 1, pl.ds(lxo, xr)], xs[d])
            for d in (2, 1, 3)
        ]
        yield

        for one in sent:
            one.wait_recv()
        put(pb, mine, xr, get(pb, mine, xr) + lx[0, lxo:lxo + xr, :]
            + lx[1, lxo:lxo + xr, :] + lx[2, lxo:lxo + xr, :])
        zo = base // 64

        def piece(p, second=0):
            return mine + ((zh + p) % 4) * zr + second * za

        def zland(ref, n):
            return ref.at[n, pl.ds(zo, za)]

        far_a = send(rows(pb, piece(2), za), zland(lz, 0), zhs[1])
        far_b = send(rows(pb, piece(2, 1), za), zland(lz, 2), zhs[3])
        near_b = send(rows(pb, piece(1, 1), za), zland(lz, 1), zhs[1])
        near_a = send(rows(pb, piece(3), za), zland(lz, 3), zhs[3])
        yield

        far_a.wait_recv()
        cz[0, zo:zo + za, :] = lz[0, zo:zo + za, :] + get(pb, piece(1), za)
        sum_a = send(zland(cz, 0), zland(lw, 0), zhs[1])
        far_b.wait_recv()
        cz[1, zo:zo + za, :] = lz[2, zo:zo + za, :] + get(pb, piece(3, 1), za)
        sum_b = send(zland(cz, 1), zland(lw, 1), zhs[3])
        yield

        near_a.wait_recv()
        near_b.wait_recv()
        sum_a.wait_recv()
        put(fb, piece(0), za, get(pb, piece(0), za) + lw[0, zo:zo + za, :] + lz[3, zo:zo + za, :])
        sum_b.wait_recv()
        put(fb, piece(0, 1), za, get(pb, piece(0, 1), za) + lw[1, zo:zo + za, :] + lz[1, zo:zo + za, :])
        up = send(rows(fb, piece(0), zr), rows(fb, piece(0), zr), zhs[1])
        down = send(rows(fb, piece(0), zr), rows(fb, piece(0), zr), zhs[3])
        yield

        up.wait_recv()
        up2 = send(rows(fb, piece(3), za), rows(fb, piece(3), za), zhs[1])
        down.wait_recv()
        down2 = send(rows(fb, piece(1, 1), za), rows(fb, piece(1, 1), za), zhs[3])
        yield

        up2.wait_recv()
        down2.wait_recv()
        sent = [send(rows(fb, mine, xr), rows(fb, mine, xr), xs[d]) for d in (2, 1, 3)]
        across = [send(rows(fb, mine, xr), rows(fb, mine, xr), sibling)]
        yield

        for d, one in zip((2, 1, 3), sent):
            one.wait_recv()
            place = own + ((x + 4 - d) % 4) * xr
            across.append(send(rows(fb, place, xr), rows(fb, place, xr), sibling))
        yield

        for one in across:
            one.wait_recv()

    def query_stage(s):
        width = WIDTHS[s]
        base = STARTS[s] * 2
        yr = width // 2
        mine = base + y * yr

        if s == 0:
            loads[2].wait()
            bt_out[...] = b_out[...].T
            loads[3].wait()
            value = dot(bt_out[...], tgr[...], ((1,), (1,)))
        else:
            if s == 1:
                loads[5].wait()
            c = STARTS[s] - TOKENS
            value = dot(bt_out[...], qout[:, c:c + width])
        for tile in range(width // LANES):
            pq[base + tile * IB:base + (tile + 1) * IB, :] = value[:, tile * LANES:(tile + 1) * LANES]
        lyo = base // 4
        sent = [
            send(rows(pq, base + ((y + d) % 4) * yr, yr), ly.at[d - 1, pl.ds(lyo, yr)], ys[d])
            for d in (2, 1, 3)
        ]
        yield

        for one in sent:
            one.wait_recv()
        put(pq, mine, yr, get(pq, mine, yr) + ly[0, lyo:lyo + yr, :]
            + ly[1, lyo:lyo + yr, :] + ly[2, lyo:lyo + yr, :])
        end = jnp.logical_or(zl == 0, zl == 3)
        middle = jnp.logical_or(zl == 1, zl == 2)
        inward = dev(zl=jnp.where(zl == 0, 1, 2))
        outward = dev(zl=jnp.where(zl == 1, 0, 3))
        over = dev(zl=3 - zl)
        block = rows(pq, mine, yr)
        done = rows(fq, mine, yr)
        to_middle = copy(block, le.at[pl.ds(lyo, yr)], inward)
        swap = copy(block, li.at[pl.ds(lyo, yr)], over)
        to_end = copy(done, done, outward)

        def when_sent(condition, one):
            def wait():
                @pl.when(condition)
                def _():
                    one.wait_send()

            unsent.append((tick[0], wait))

        @pl.when(end)
        def _():
            to_middle.start()

        when_sent(end, to_middle)
        yield

        @pl.when(middle)
        def _():
            to_middle.wait_recv()
            put(pq, mine, yr, get(pq, mine, yr) + le[lyo:lyo + yr, :])
            swap.start()

        when_sent(middle, swap)
        yield

        @pl.when(middle)
        def _():
            swap.wait_recv()
            put(fq, mine, yr, get(pq, mine, yr) + li[lyo:lyo + yr, :])
            to_end.start()

        when_sent(middle, to_end)
        yield

        @pl.when(end)
        def _():
            to_end.wait_recv()

        sent = [send(done, done, ys[d]) for d in (2, 1, 3)]
        yield

        for one in sent:
            one.wait_recv()

    def tiles(ref, base, count, size):
        return jnp.concatenate([ref[base + n * size:base + (n + 1) * size, :] for n in range(count)], axis=1)

    def make_scaled():
        g = tiles(fq, 0, 2, IB)
        a_hi, a_lo = split(tiles(fb, 0, 2, JB))
        g_hi, g_lo = split(g)
        loads[7].wait()
        zero = jnp.zeros_like(g_hi)
        total = None
        nt = ((1,), (1,))
        for n in range(EXAMPLES):
            mask = jnp.broadcast_to(eid[...] == n, (IB, TOKENS))
            high, low = jnp.where(mask, g_hi, zero), jnp.where(mask, g_lo, zero)
            scaled = (dot(high, a_hi, nt) + dot(high, a_lo, nt) + dot(low, a_hi, nt)) * inv[...]
            total = scaled if total is None else total + scaled
            hi, lo = split(scaled)
            s_hi[n] = hi
            s_lo[n] = lo
        o_total[...] = total.astype(jnp.bfloat16)

    def influence_of(s):
        width = WIDTHS[s]
        c = STARTS[s] - TOKENS
        count = width // LANES
        for first in range(0, count, 2):
            r_hi, r_lo = split(tiles(fb, STARTS[s] * 4 + first * JB, 2, JB))
            out = tiles(fq, STARTS[s] * 2 + first * IB, 2, IB)
            at = c + first * LANES
            for n in range(EXAMPLES):
                weighted = dot(s_hi[n], r_hi) + dot(s_hi[n], r_lo) + dot(s_lo[n], r_hi)
                part[n:n + 1, at:at + 2 * LANES] = jnp.sum(weighted * out, axis=0, keepdims=True)

    part[...] = jnp.zeros_like(part)
    running = []
    waiting = list(range(STAGES))
    while waiting or running:
        if waiting:
            s = waiting.pop(0)
            running.append([s, [basis_stage(s), query_stage(s)]])
        ended = []
        for item in running:
            alive = []
            for step in item[1]:
                try:
                    next(step)
                    alive.append(step)
                except StopIteration:
                    pass
            item[1] = alive
            if not alive:
                ended.append(item[0])
        running = [item for item in running if item[1]]
        if tick[0] == STAGES - 1:
            loads[6].wait()
            inv[...] = 1.0 / (eig[...] + DAMPING)
        for s in ended:
            if s == 0:
                make_scaled()
            else:
                influence_of(s)
        tick[0] += 1
        drain(tick[0] - 2)

    lane = lax.broadcasted_iota(jnp.int32, (QC, LANES), 1)
    row = lax.broadcasted_iota(jnp.int32, (QC, LANES), 0)
    value = select_dot(part[...], (row // RANK == lane).astype(jnp.bfloat16))

    def reduce(value, slots, index, targets):
        slots[index] = value
        sent = [send(slots.at[index], slots.at[index], target) for target in targets]
        for one in sent:
            one.wait_recv()
        total = slots[0]
        for n in range(1, slots.shape[0]):
            total = total + slots[n]
        return total

    value = reduce(value, ar_c, core, [sibling])
    value = reduce(value, ar_x, x, xs[1:])
    value = reduce(value, ar_y, y, ys[1:])
    value = reduce(value, ar_l, zl, zls[1:])
    value = reduce(value, ar_h, zh, zhs[1:])

    loads[8].wait()
    query_row = lax.broadcasted_iota(jnp.int32, (QUERIES, LANES), 1)
    table = (jnp.broadcast_to(tid[...], (QUERIES, LANES)) == query_row).astype(jnp.float32)
    counts = jnp.sum(table, axis=0, keepdims=True)
    padded = jnp.concatenate([table, jnp.zeros((LANES - QUERIES, LANES), jnp.float32)], axis=0)
    tasks = select_dot(value, padded.astype(jnp.bfloat16))
    o_inf[...] = value[:EXAMPLES, :QUERIES]
    o_task[...] = tasks[:EXAMPLES, :TASKS] / counts[:, :TASKS]
    drain(tick[0] + 1)


def shards(train_inputs, train_grads, example_ids, task_ids, basis_in, basis_out, eigenvalues, query_in, query_out):
    vm = pltpu.VMEM
    f32, bf16 = jnp.float32, jnp.bfloat16
    example_ids = example_ids.reshape(1, TOKENS)
    loaded = [
        vm(a.shape, a.dtype)
        for a in (train_inputs, train_grads, example_ids, task_ids, basis_in, basis_out, eigenvalues, query_in, query_out)
    ]
    scratch = loaded + [
        vm((JB, IB), bf16),
        vm((IB, JB), bf16),
        vm((IB, JB), f32),
        vm((TOTAL * 4, LANES), f32),
        vm((TOTAL * 4, LANES), f32),
        vm((TOTAL * 2, LANES), f32),
        vm((3, TOTAL // 2, LANES), f32),
        vm((4, TOTAL // 16, LANES), f32),
        vm((2, TOTAL // 16, LANES), f32),
        vm((2, TOTAL // 16, LANES), f32),
        vm((TOTAL * 2, LANES), f32),
        vm((TOTAL * 2, LANES), f32),
        vm((3, TOTAL // 2, LANES), f32),
        vm((TOTAL // 2, LANES), f32),
        vm((TOTAL // 2, LANES), f32),
        vm((EXAMPLES, IB, JB), bf16),
        vm((EXAMPLES, IB, JB), bf16),
        vm((8, QC), f32),
        vm((2, 8, LANES), f32),
        vm((4, 8, LANES), f32),
        vm((4, 8, LANES), f32),
        vm((4, 8, LANES), f32),
        vm((4, 8, LANES), f32),
        pltpu.SemaphoreType.DMA((COPIES,)),
        pltpu.SemaphoreType.DMA((COPIES,)),
        pltpu.SemaphoreType.DMA((9,)),
    ]
    return pl.pallas_call(
        kernel,
        out_shape=(
            jax.ShapeDtypeStruct((IB, JB), bf16),
            jax.ShapeDtypeStruct((EXAMPLES, QUERIES), f32),
            jax.ShapeDtypeStruct((EXAMPLES, TASKS), f32),
        ),
        in_specs=[pl.BlockSpec(memory_space=pl.ANY)] * 9,
        out_specs=[pl.BlockSpec(memory_space=pltpu.VMEM)] * 3,
        scratch_shapes=scratch,
        compiler_params=pltpu.CompilerParams(
            collective_id=0, has_side_effects=True, vmem_limit_bytes=52 * 2**20
        ),
        name="influence",
    )(train_inputs, train_grads, example_ids, task_ids, basis_in, basis_out, eigenvalues, query_in, query_out)


def solution(mesh):
    in_specs = (
        P(None, "basis"),
        P(None, "query"),
        P(),
        P(),
        P("basis", "query"),
        P("query", "basis"),
        P("basis", "query"),
        P("basis", None),
        P("query", None),
    )
    out_specs = (P("basis", "query"), P(), P())
    return jax.shard_map(shards, mesh=mesh, in_specs=in_specs, out_specs=out_specs, check_vma=False)
```

time: 698 us -> 123 us (0.18)
  waiting for transfers between devices: 549 us -> 0 us
  Pallas kernels: 0 us -> 113 us
  blocking collectives: 107 us -> 0 us
  matrix products: 24.3 us -> 0 us
  between operations: 14.2 us -> 0.65 us
    psum x2 -> x0, waiting for transfers between devices: 549 us -> none  [the longest x1 380 us: shards(): rot_inputs, rot_query_in = lax.psum((input_term, factor_in), 'basis')]
    pallas_call x0 -> x1, Pallas kernels: none -> 113 us  [shards(): pl.pallas_call(kernel, out_shape=(jax.ShapeDtypeStruct((IB, JB), bf16), j...]
    psum x1 -> x0, blocking collectives: 107 us -> none  [shards(): influence = lax.psum(partial_value, ('basis', 'query'))]
    dot_general x13 -> x0, matrix products: 24.3 us -> none  [the longest x4 11.7 us: shards(): jnp.dot(scaled, rot_query_in, precision=lax.Precision.HIGHEST, preferred_...]
  transfers between devices with their start and end apart: 2 -> 0, of which waited for: 2 -> 0; matrix products, arithmetic and copies ran while one was open for 0% -> 0% of each run, Pallas kernels for 0% -> 0%
where the time goes in v1:
time: 123 us; the launch traced here: 122 us
  Pallas kernels  113 us (92%)
  local copies, waits for them, and re-layouts  8.07 us (7%)
    pallas_call x1, Pallas kernels, shards(): pl.pallas_call(kernel, out_shape=(jax.ShapeDtypeStruct((IB, JB), bf16), j...  113 us
    unnamed x16, local copies, waits for them, and re-layouts  8.07 us

profile of v1, /device:TPU:1, one launch (start us, length us, event | category | flops | bytes accessed | tf_op | source)
XLA Modules:
  0.0 122.2 jit_solution(1701080928026000631)
XLA Ops:
  0.6 0.7 copy.12.h_tid
  1.4 0.0 copy-start
  1.4 1.0 copy-done
  2.4 0.0 copy-start.1
  2.4 0.9 copy-done.1
  3.4 0.0 copy-start.2
  3.4 0.9 copy-done.2
  4.3 0.0 copy-start.3
  4.3 0.9 copy-done.3
  5.3 0.0 copy-start.4
  5.3 0.9 copy-done.4
  6.2 0.0 copy-start.5
  6.2 0.7 copy-done.5
  6.8 113.5 %influence.1 = (bf16[256,512]{1,0:T(8,128)(2,1)S(1)}, f32[4,48]{1,0:T(4,128)S(1)}, f32[4,16]{1,0:T(4,128)S(1)}) custom-call(bf16[256,256]{1,0:T(8,128)(2,1)S(1)} %copy-done.4, bf16[256,512]{1,0:T(8,128)(2,1)S(1)} %copy-done.1, s32[1,256]{1,0:T(1,128)S(1)} %bitcast.1, s32[48,1]{1,0:T(8,128)S(1)} %copy.12.h_tid, bf16[256,512]{1,0:T(8,128)(2,1)S(1)} %copy-done.2, ...), custom_call_target="tpu_custom_call" | custom-call | tf_op jit(solution)/shard_map/influence/pallas_call | solution.py:419
  120.3 0.7 copy.16
  121.1 0.6 copy.17
  121.6 0.6 copy.18
Async XLA Ops:
  1.4 1.0 copy-start
  2.4 0.9 copy-start.1
  3.4 0.9 copy-start.2
  4.3 0.9 copy-start.3
  5.3 0.9 copy-start.4
  6.2 0.7 copy-start.5

commit v2 on v1

--- a/solution.py
+++ b/solution.py
@@ -18,12 +18,23 @@
 IB = 256
 LANES = 128
 
-WIDTHS = (256, 512, 512, 512)
+WIDTHS = (256, 384, 384, 384, 384)
 STARTS = tuple(sum(WIDTHS[:s]) for s in range(len(WIDTHS)))
 STAGES = len(WIDTHS)
 TOTAL = sum(WIDTHS)
+ORDER = (
+    (0, 0), (1, 1), (1, 4), (0, 0), (0, 2), (0, 2), (0, 4), (0, 0), (0, 4), (1, 0),
+    (0, 1), (0, 3), (1, 1), (1, 4), (0, 2), (1, 2), (0, 1), (0, 0), (1, 0), (1, 1),
+    (0, 4), (0, 3), (1, 4), (0, 2), (0, 0), (1, 3), (0, 1), (1, 4), (0, 4), (0, 3),
+    (1, 0), (0, 2), (0, 1), (1, 4), (1, 0), (0, 4), (0, 0), (1, 2), (1, 3), (0, 3),
+    (0, 2), (0, 1), (1, 0), (1, 4), (0, 0), (1, 1), (1, 2), (1, 3), (0, 4), (0, 3),
+    (0, 2), (0, 1), (0, 0), (1, 1), (1, 2), (0, 4), (0, 3), (0, 1), (0, 0), (1, 3),
+    (1, 2), (1, 0), (2, 0), (0, 3), (1, 3), (1, 1), (0, 4), (0, 1), (0, 2), (0, 4),
+    (2, 4), (1, 2), (0, 1), (2, 1), (0, 3), (0, 2), (2, 2), (1, 3), (0, 3), (2, 3),
+)
 MESH = pl.DeviceIdType.MESH
-COPIES = 160
+COPIES = 200
+EARLY = 1
 
 
 def dot(a, b, contract=((1,), (0,))):
@@ -35,10 +46,10 @@
     return high, (value - high.astype(jnp.float32)).astype(jnp.bfloat16)
 
 
-def select_dot(value, table):
+def select_dot(value, table, contract=((1,), (0,))):
     high, rest = split(value)
     mid = (value - high.astype(jnp.float32) - rest.astype(jnp.float32)).astype(jnp.bfloat16)
-    return dot(high, table) + dot(rest, table) + dot(mid, table)
+    return dot(high, table, contract) + dot(rest, table, contract) + dot(mid, table, contract)
 
 
 def kernel(
@@ -47,7 +58,7 @@
     tin, tgr, eid, tid, b_in, b_out, eig, qin, qout,
     bt_in, bt_out, inv,
     pb, fb, ls, lx, lz, lw, cz, pq, fq, ly, le, li,
-    s_hi, s_lo, part, ar_c, ar_x, ar_y, ar_l, ar_h,
+    s_hi, s_lo, part, ar_c, ar_p, ar_z,
     send_sem, recv_sem, load_sem,
 ):
     basis, query = lax.axis_index("basis"), lax.axis_index("query")
@@ -61,21 +72,25 @@
     xs = [None] + [dev(x=(x + d) % 4) for d in (1, 2, 3)]
     ys = [None] + [dev(y=(y + d) % 4) for d in (1, 2, 3)]
     zhs = [None] + [dev(zh=(zh + d) % 4) for d in (1, 2, 3)]
-    zls = [None] + [dev(zl=(zl + d) % 4) for d in (1, 2, 3)]
-
-    loads = []
-    for n, (src, dst) in enumerate((
+
+    pairs = (
         (h_bin, b_in), (h_tin, tin), (h_bout, b_out), (h_tgr, tgr), (h_qin, qin),
         (h_qout, qout), (h_eig, eig), (h_eid, eid), (h_tid, tid),
-    )):
-        load = pltpu.make_async_copy(src, dst, load_sem.at[n])
+    )
+    loads = [pltpu.make_async_copy(src, dst, load_sem.at[n]) for n, (src, dst) in enumerate(pairs)]
+    for load in loads[:4]:
         load.start()
-        loads.append(load)
 
     barrier = pltpu.get_barrier_semaphore()
-    peers = [sibling] + xs[1:] + ys[1:] + zhs[1:] + zls[1:]
+    z = zh * 4 + zl
+    plane = [dev(x=(x + a) % 4, y=(y + b) % 4) for a in (2, 1, 3, 0) for b in (2, 1, 3, 0) if a or b]
+    far = sorted(range(1, 16), key=lambda d: abs(d - 8))
+    column = [dev(zh=((z + d) % 16) // 4, zl=(z + d) % 4) for d in far]
+    peers = column + plane + [sibling]
     for peer in peers:
         pl.semaphore_signal(barrier, inc=1, device_id=peer, device_id_type=MESH)
+    for load in loads[4:]:
+        load.start()
 
     made = [0]
 
@@ -124,14 +139,12 @@
             loads[1].wait()
             value = dot(bt_in[...], tin[...], ((1,), (1,)))
         else:
-            if s == 1:
-                loads[4].wait()
             c = STARTS[s] - TOKENS
             value = dot(bt_in[...], qin[:, c:c + width])
         for tile in range(width // LANES):
             pb[base + tile * JB:base + (tile + 1) * JB, :] = value[:, tile * LANES:(tile + 1) * LANES]
-        if s == 0:
-            pl.semaphore_wait(barrier, len(peers))
+        yield
+
         landing = ls.at[pl.ds(base // 2, half)]
         pair = send(rows(pb, base + (1 - core) * half, half), landing, sibling)
         yield
@@ -214,12 +227,12 @@
             loads[3].wait()
             value = dot(bt_out[...], tgr[...], ((1,), (1,)))
         else:
-            if s == 1:
-                loads[5].wait()
             c = STARTS[s] - TOKENS
             value = dot(bt_out[...], qout[:, c:c + width])
         for tile in range(width // LANES):
             pq[base + tile * IB:base + (tile + 1) * IB, :] = value[:, tile * LANES:(tile + 1) * LANES]
+        yield
+
         lyo = base // 4
         sent = [
             send(rows(pq, base + ((y + d) % 4) * yr, yr), ly.at[d - 1, pl.ds(lyo, yr)], ys[d])
@@ -311,43 +324,37 @@
         c = STARTS[s] - TOKENS
         count = width // LANES
         for first in range(0, count, 2):
-            r_hi, r_lo = split(tiles(fb, STARTS[s] * 4 + first * JB, 2, JB))
-            out = tiles(fq, STARTS[s] * 2 + first * IB, 2, IB)
+            many = min(2, count - first)
+            r_hi, r_lo = split(tiles(fb, STARTS[s] * 4 + first * JB, many, JB))
+            out = tiles(fq, STARTS[s] * 2 + first * IB, many, IB)
             at = c + first * LANES
             for n in range(EXAMPLES):
                 weighted = dot(s_hi[n], r_hi) + dot(s_hi[n], r_lo) + dot(s_lo[n], r_hi)
-                part[n:n + 1, at:at + 2 * LANES] = jnp.sum(weighted * out, axis=0, keepdims=True)
+                part[n:n + 1, at:at + many * LANES] = jnp.sum(weighted * out, axis=0, keepdims=True)
 
     part[...] = jnp.zeros_like(part)
-    running = []
-    waiting = list(range(STAGES))
-    while waiting or running:
-        if waiting:
-            s = waiting.pop(0)
-            running.append([s, [basis_stage(s), query_stage(s)]])
-        ended = []
-        for item in running:
-            alive = []
-            for step in item[1]:
-                try:
-                    next(step)
-                    alive.append(step)
-                except StopIteration:
-                    pass
-            item[1] = alive
-            if not alive:
-                ended.append(item[0])
-        running = [item for item in running if item[1]]
-        if tick[0] == STAGES - 1:
+    begun = set()
+    chains = [[basis_stage(s) for s in range(STAGES)], [query_stage(s) for s in range(STAGES)]]
+    for s in range(EARLY):
+        next(chains[0][s])
+        next(chains[1][s])
+    pl.semaphore_wait(barrier, len(peers))
+    loads[4].wait()
+    loads[5].wait()
+    for kind, s in ORDER:
+        if kind < 2 and s >= EARLY and (kind, s) not in begun:
+            next(chains[kind][s])
+            begun.add((kind, s))
+        if kind < 2:
+            next(chains[kind][s], None)
+        elif s == 0:
             loads[6].wait()
             inv[...] = 1.0 / (eig[...] + DAMPING)
-        for s in ended:
-            if s == 0:
-                make_scaled()
-            else:
-                influence_of(s)
+            make_scaled()
+        else:
+            influence_of(s)
         tick[0] += 1
-        drain(tick[0] - 2)
+        drain(tick[0] - 16)
 
     lane = lax.broadcasted_iota(jnp.int32, (QC, LANES), 1)
     row = lax.broadcasted_iota(jnp.int32, (QC, LANES), 0)
@@ -364,19 +371,17 @@
         return total
 
     value = reduce(value, ar_c, core, [sibling])
-    value = reduce(value, ar_x, x, xs[1:])
-    value = reduce(value, ar_y, y, ys[1:])
-    value = reduce(value, ar_l, zl, zls[1:])
-    value = reduce(value, ar_h, zh, zhs[1:])
+    value = reduce(value, ar_p, x * 4 + y, plane)
+    value = reduce(value, ar_z, z, column)
 
     loads[8].wait()
-    query_row = lax.broadcasted_iota(jnp.int32, (QUERIES, LANES), 1)
-    table = (jnp.broadcast_to(tid[...], (QUERIES, LANES)) == query_row).astype(jnp.float32)
-    counts = jnp.sum(table, axis=0, keepdims=True)
-    padded = jnp.concatenate([table, jnp.zeros((LANES - QUERIES, LANES), jnp.float32)], axis=0)
-    tasks = select_dot(value, padded.astype(jnp.bfloat16))
+    task = lax.broadcasted_iota(jnp.int32, (TASKS, QUERIES), 0)
+    table = (jnp.broadcast_to(tid[...], (TASKS, QUERIES)) == task).astype(jnp.bfloat16)
+    nt = ((1,), (1,))
+    counts = dot(jnp.ones((8, QUERIES), jnp.bfloat16), table, nt)
+    tasks = select_dot(value[:, :QUERIES], table, nt)
     o_inf[...] = value[:EXAMPLES, :QUERIES]
-    o_task[...] = tasks[:EXAMPLES, :TASKS] / counts[:, :TASKS]
+    o_task[...] = tasks[:EXAMPLES] / counts[:EXAMPLES]
     drain(tick[0] + 1)
 
 
@@ -384,6 +389,7 @@
     vm = pltpu.VMEM
     f32, bf16 = jnp.float32, jnp.bfloat16
     example_ids = example_ids.reshape(1, TOKENS)
+    task_ids = task_ids.reshape(1, QUERIES)
     loaded = [
         vm(a.shape, a.dtype)
         for a in (train_inputs, train_grads, example_ids, task_ids, basis_in, basis_out, eigenvalues, query_in, query_out)
@@ -408,10 +414,8 @@
         vm((EXAMPLES, IB, JB), bf16),
         vm((8, QC), f32),
         vm((2, 8, LANES), f32),
-        vm((4, 8, LANES), f32),
-        vm((4, 8, LANES), f32),
-        vm((4, 8, LANES), f32),
-        vm((4, 8, LANES), f32),
+        vm((16, 8, LANES), f32),
+        vm((16, 8, LANES), f32),
         pltpu.SemaphoreType.DMA((COPIES,)),
         pltpu.SemaphoreType.DMA((COPIES,)),
         pltpu.SemaphoreType.DMA((9,)),
@@ -427,7 +431,7 @@
         out_specs=[pl.BlockSpec(memory_space=pltpu.VMEM)] * 3,
         scratch_shapes=scratch,
         compiler_params=pltpu.CompilerParams(
-            collective_id=0, has_side_effects=True, vmem_limit_bytes=52 * 2**20
+            collective_id=0, has_side_effects=True, vmem_limit_bytes=62 * 2**20
         ),
         name="influence",
     )(train_inputs, train_grads, example_ids, task_ids, basis_in, basis_out, eigenvalues, query_in, query_out)

time: 123 us -> 115 us (0.935)
  Pallas kernels: 113 us -> 109 us
  local copies, waits for them, and re-layouts: 8.07 us -> 4.18 us
    pallas_call x1, Pallas kernels: 113 us -> 109 us  [shards(): pl.pallas_call(kernel, out_shape=(jax.ShapeDtypeStruct((IB, JB), bf16), j...]
    unnamed x16 -> x3, local copies, waits for them, and re-layouts: 8.07 us -> 4.18 us
where the time goes in v2:
time: 115 us; the launch traced here: 114 us
  Pallas kernels  109 us (95%)
  local copies, waits for them, and re-layouts  4.18 us (4%)
    pallas_call x1, Pallas kernels, shards(): pl.pallas_call(kernel, out_shape=(jax.ShapeDtypeStruct((IB, JB), bf16), j...  109 us
    unnamed x3, local copies, waits for them, and re-layouts  4.18 us

profile of v2, /device:TPU:1, one launch (start us, length us, event | category | flops | bytes accessed | tf_op | source)
XLA Modules:
  0.0 114.3 jit_solution(3780585678678741366)
XLA Ops:
  0.6 109.5 %influence.1 = (bf16[256,512]{1,0:T(8,128)(2,1)}, f32[4,48]{1,0:T(4,128)}, f32[4,16]{1,0:T(4,128)}) custom-call(bf16[256,256]{1,0:T(8,128)(2,1)} %h_tin.1, bf16[256,512]{1,0:T(8,128)(2,1)} %h_tgr.1, s32[1,256]{1,0:T(1,128)} %bitcast.2, s32[1,48]{1,0:T(1,128)} %bitcast.3, bf16[256,512]{1,0:T(8,128)(2,1)} %h_bin.1, bf16[512,256]{1,0:T(8,128)(2,1)} %h_bout.1, ...), custom_call_target="tpu_custom_call" | custom-call | tf_op jit(solution)/shard_map/influence/pallas_call | solution.py:423
  110.1 1.7 %copy.15 = bf16[256,512]{1,0:T(8,128)(2,1)} copy(bf16[256,512]{1,0:T(8,128)(2,1)} %get-tuple-element.6) | data formatting | bytes 524288
  111.8 1.2 %copy.16 = f32[4,48]{1,0:T(4,128)} copy(f32[4,48]{1,0:T(4,128)} %get-tuple-element.7) | data formatting | bytes 1536
  113.1 1.3 %copy.17 = f32[4,16]{1,0:T(4,128)} copy(f32[4,16]{1,0:T(4,128)} %get-tuple-element.8) | data formatting | bytes 512

commit v3 on v2

--- a/solution.py
+++ b/solution.py
@@ -18,23 +18,27 @@
 IB = 256
 LANES = 128
 
-WIDTHS = (256, 384, 384, 384, 384)
+WIDTHS = (256, 256, 256, 256, 256, 256, 256)
 STARTS = tuple(sum(WIDTHS[:s]) for s in range(len(WIDTHS)))
 STAGES = len(WIDTHS)
 TOTAL = sum(WIDTHS)
 ORDER = (
-    (0, 0), (1, 1), (1, 4), (0, 0), (0, 2), (0, 2), (0, 4), (0, 0), (0, 4), (1, 0),
-    (0, 1), (0, 3), (1, 1), (1, 4), (0, 2), (1, 2), (0, 1), (0, 0), (1, 0), (1, 1),
-    (0, 4), (0, 3), (1, 4), (0, 2), (0, 0), (1, 3), (0, 1), (1, 4), (0, 4), (0, 3),
-    (1, 0), (0, 2), (0, 1), (1, 4), (1, 0), (0, 4), (0, 0), (1, 2), (1, 3), (0, 3),
-    (0, 2), (0, 1), (1, 0), (1, 4), (0, 0), (1, 1), (1, 2), (1, 3), (0, 4), (0, 3),
-    (0, 2), (0, 1), (0, 0), (1, 1), (1, 2), (0, 4), (0, 3), (0, 1), (0, 0), (1, 3),
-    (1, 2), (1, 0), (2, 0), (0, 3), (1, 3), (1, 1), (0, 4), (0, 1), (0, 2), (0, 4),
-    (2, 4), (1, 2), (0, 1), (2, 1), (0, 3), (0, 2), (2, 2), (1, 3), (0, 3), (2, 3),
+    (0, 3), (1, 0), (0, 2), (1, 1), (0, 3), (0, 0), (0, 5), (0, 0), (1, 4), (1, 5),
+    (0, 3), (0, 6), (0, 4), (0, 5), (1, 2), (0, 1), (1, 0), (1, 3), (0, 0), (0, 2),
+    (1, 1), (0, 3), (0, 1), (1, 0), (0, 5), (0, 6), (1, 5), (1, 4), (0, 0), (0, 2),
+    (0, 4), (1, 0), (0, 3), (1, 1), (0, 1), (0, 0), (0, 5), (0, 6), (1, 2), (1, 1),
+    (0, 3), (0, 2), (1, 6), (0, 1), (0, 5), (1, 2), (0, 0), (0, 4), (1, 4), (0, 6),
+    (1, 3), (0, 3), (0, 1), (1, 0), (1, 2), (1, 5), (0, 2), (1, 3), (0, 5), (0, 0),
+    (0, 6), (1, 2), (1, 6), (0, 4), (0, 1), (1, 1), (1, 5), (1, 4), (0, 2), (0, 5),
+    (1, 3), (0, 3), (1, 6), (0, 6), (0, 4), (0, 1), (1, 2), (1, 5), (1, 1), (0, 0),
+    (1, 6), (0, 5), (1, 3), (0, 3), (0, 6), (0, 5), (0, 0), (0, 2), (0, 4), (1, 4),
+    (0, 1), (1, 6), (1, 0), (2, 0), (0, 4), (1, 5), (2, 5), (0, 1), (2, 1), (0, 6),
+    (0, 2), (1, 3), (2, 3), (0, 6), (1, 6), (2, 6), (0, 4), (0, 2), (2, 2), (1, 4),
+    (0, 4), (2, 4),
 )
 MESH = pl.DeviceIdType.MESH
-COPIES = 200
-EARLY = 1
+COPIES = 264
+EARLY = 7
 
 
 def dot(a, b, contract=((1,), (0,))):
@@ -56,7 +60,7 @@
     h_tin, h_tgr, h_eid, h_tid, h_bin, h_bout, h_eig, h_qin, h_qout,
     o_total, o_inf, o_task,
     tin, tgr, eid, tid, b_in, b_out, eig, qin, qout,
-    bt_in, bt_out, inv,
+    bt_in, bt_out, inv, total_bf,
     pb, fb, ls, lx, lz, lw, cz, pq, fq, ly, le, li,
     s_hi, s_lo, part, ar_c, ar_p, ar_z,
     send_sem, recv_sem, load_sem,
@@ -203,17 +207,14 @@
         up2.wait_recv()
         down2.wait_recv()
         sent = [send(rows(fb, mine, xr), rows(fb, mine, xr), xs[d]) for d in (2, 1, 3)]
-        across = [send(rows(fb, mine, xr), rows(fb, mine, xr), sibling)]
-        yield
-
-        for d, one in zip((2, 1, 3), sent):
+        yield
+
+        for one in sent:
             one.wait_recv()
-            place = own + ((x + 4 - d) % 4) * xr
-            across.append(send(rows(fb, place, xr), rows(fb, place, xr), sibling))
-        yield
-
-        for one in across:
-            one.wait_recv()
+        across = send(rows(fb, own, half), rows(fb, own, half), sibling)
+        yield
+
+        across.wait_recv()
 
     def query_stage(s):
         width = WIDTHS[s]
@@ -300,6 +301,8 @@
 
     def tiles(ref, base, count, size):
         return jnp.concatenate([ref[base + n * size:base + (n + 1) * size, :] for n in range(count)], axis=1)
+
+    store_total = pltpu.make_async_copy(total_bf, o_total, load_sem.at[9])
 
     def make_scaled():
         g = tiles(fq, 0, 2, IB)
@@ -317,7 +320,8 @@
             hi, lo = split(scaled)
             s_hi[n] = hi
             s_lo[n] = lo
-        o_total[...] = total.astype(jnp.bfloat16)
+        total_bf[...] = total.astype(jnp.bfloat16)
+        store_total.start()
 
     def influence_of(s):
         width = WIDTHS[s]
@@ -336,11 +340,12 @@
     begun = set()
     chains = [[basis_stage(s) for s in range(STAGES)], [query_stage(s) for s in range(STAGES)]]
     for s in range(EARLY):
+        if s == 1:
+            loads[4].wait()
+            loads[5].wait()
         next(chains[0][s])
         next(chains[1][s])
     pl.semaphore_wait(barrier, len(peers))
-    loads[4].wait()
-    loads[5].wait()
     for kind, s in ORDER:
         if kind < 2 and s >= EARLY and (kind, s) not in begun:
             next(chains[kind][s])
@@ -383,6 +388,12 @@
     o_inf[...] = value[:EXAMPLES, :QUERIES]
     o_task[...] = tasks[:EXAMPLES] / counts[:EXAMPLES]
     drain(tick[0] + 1)
+    store_total.wait()
+
+
+def finish(*refs):
+    for src, dst in zip(refs[:3], refs[3:]):
+        dst[...] = src[...]
 
 
 def shards(train_inputs, train_grads, example_ids, task_ids, basis_in, basis_out, eigenvalues, query_in, query_out):
@@ -398,6 +409,7 @@
         vm((JB, IB), bf16),
         vm((IB, JB), bf16),
         vm((IB, JB), f32),
+        vm((IB, JB), bf16),
         vm((TOTAL * 4, LANES), f32),
         vm((TOTAL * 4, LANES), f32),
         vm((TOTAL * 2, LANES), f32),
@@ -418,23 +430,32 @@
         vm((16, 8, LANES), f32),
         pltpu.SemaphoreType.DMA((COPIES,)),
         pltpu.SemaphoreType.DMA((COPIES,)),
-        pltpu.SemaphoreType.DMA((9,)),
+        pltpu.SemaphoreType.DMA((10,)),
     ]
-    return pl.pallas_call(
+    shapes = (
+        jax.ShapeDtypeStruct((IB, JB), bf16),
+        jax.ShapeDtypeStruct((EXAMPLES, QUERIES), f32),
+        jax.ShapeDtypeStruct((EXAMPLES, TASKS), f32),
+    )
+    results = pl.pallas_call(
         kernel,
-        out_shape=(
-            jax.ShapeDtypeStruct((IB, JB), bf16),
-            jax.ShapeDtypeStruct((EXAMPLES, QUERIES), f32),
-            jax.ShapeDtypeStruct((EXAMPLES, TASKS), f32),
-        ),
+        out_shape=shapes,
         in_specs=[pl.BlockSpec(memory_space=pl.ANY)] * 9,
-        out_specs=[pl.BlockSpec(memory_space=pltpu.VMEM)] * 3,
+        out_specs=[pl.BlockSpec(memory_space=pl.ANY)] + [pl.BlockSpec(memory_space=pltpu.VMEM)] * 2,
         scratch_shapes=scratch,
         compiler_params=pltpu.CompilerParams(
             collective_id=0, has_side_effects=True, vmem_limit_bytes=62 * 2**20
         ),
         name="influence",
     )(train_inputs, train_grads, example_ids, task_ids, basis_in, basis_out, eigenvalues, query_in, query_out)
+    return pl.pallas_call(
+        finish,
+        out_shape=shapes,
+        in_specs=[pl.BlockSpec(memory_space=pltpu.VMEM)] * 3,
+        out_specs=[pl.BlockSpec(memory_space=pltpu.VMEM)] * 3,
+        compiler_params=pltpu.CompilerParams(vmem_limit_bytes=62 * 2**20),
+        name="finish",
+    )(*results)
 
 
 def solution(mesh):

time: 115 us -> 107 us (0.930)
  local copies, waits for them, and re-layouts: 4.18 us -> 0 us
  Pallas kernels: 109 us -> 107 us
    unnamed x3 -> x0, local copies, waits for them, and re-layouts: 4.18 us -> none
    pallas_call x1 -> x2, Pallas kernels: 109 us -> 107 us  [the longest x1 105 us: shards(): pl.pallas_call(kernel, out_shape=shapes, in_specs=[pl.BlockSpec(memory_sp...]
where the time goes in v3:
time: 107 us
  Pallas kernels  107 us (100%)
    pallas_call x1, Pallas kernels, shards(): pl.pallas_call(kernel, out_shape=shapes, in_specs=[pl.BlockSpec(memory_sp...  105 us

profile of v3, /device:TPU:1, one launch (start us, length us, event | category | flops | bytes accessed | tf_op | source)
XLA Modules:
  0.0 107.3 jit_solution(9222952125076383274)
XLA Ops:
  0.6 105.0 %influence.1 = (bf16[256,512]{1,0:T(8,128)(2,1)}, f32[4,48]{1,0:T(4,128)}, f32[4,16]{1,0:T(4,128)}) custom-call(bf16[256,256]{1,0:T(8,128)(2,1)} %h_tin.1, bf16[256,512]{1,0:T(8,128)(2,1)} %h_tgr.1, s32[1,256]{1,0:T(1,128)} %bitcast.2, s32[1,48]{1,0:T(1,128)} %bitcast.3, bf16[256,512]{1,0:T(8,128)(2,1)} %h_bin.1, bf16[512,256]{1,0:T(8,128)(2,1)} %h_bout.1, ...), custom_call_target="tpu_custom_call" | custom-call | tf_op jit(solution)/shard_map/influence/pallas_call | solution.py:440
  105.6 1.7 %finish.1 = (bf16[256,512]{1,0:T(8,128)(2,1)}, f32[4,48]{1,0:T(4,128)}, f32[4,16]{1,0:T(4,128)}) custom-call(bf16[256,512]{1,0:T(8,128)(2,1)} %get-tuple-element.6.refs_0_, f32[4,48]{1,0:T(4,128)} %get-tuple-element.7.refs_1_, f32[4,16]{1,0:T(4,128)} %get-tuple-element.8.refs_2_), custom_call_target="tpu_custom_call" | custom-call | tf_op jit(solution)/shard_map/finish/pallas_call | solution.py:451

commit v4 on v3

--- a/solution.py
+++ b/solution.py
@@ -23,18 +23,18 @@
 STAGES = len(WIDTHS)
 TOTAL = sum(WIDTHS)
 ORDER = (
-    (0, 3), (1, 0), (0, 2), (1, 1), (0, 3), (0, 0), (0, 5), (0, 0), (1, 4), (1, 5),
-    (0, 3), (0, 6), (0, 4), (0, 5), (1, 2), (0, 1), (1, 0), (1, 3), (0, 0), (0, 2),
-    (1, 1), (0, 3), (0, 1), (1, 0), (0, 5), (0, 6), (1, 5), (1, 4), (0, 0), (0, 2),
-    (0, 4), (1, 0), (0, 3), (1, 1), (0, 1), (0, 0), (0, 5), (0, 6), (1, 2), (1, 1),
-    (0, 3), (0, 2), (1, 6), (0, 1), (0, 5), (1, 2), (0, 0), (0, 4), (1, 4), (0, 6),
-    (1, 3), (0, 3), (0, 1), (1, 0), (1, 2), (1, 5), (0, 2), (1, 3), (0, 5), (0, 0),
-    (0, 6), (1, 2), (1, 6), (0, 4), (0, 1), (1, 1), (1, 5), (1, 4), (0, 2), (0, 5),
-    (1, 3), (0, 3), (1, 6), (0, 6), (0, 4), (0, 1), (1, 2), (1, 5), (1, 1), (0, 0),
-    (1, 6), (0, 5), (1, 3), (0, 3), (0, 6), (0, 5), (0, 0), (0, 2), (0, 4), (1, 4),
-    (0, 1), (1, 6), (1, 0), (2, 0), (0, 4), (1, 5), (2, 5), (0, 1), (2, 1), (0, 6),
-    (0, 2), (1, 3), (2, 3), (0, 6), (1, 6), (2, 6), (0, 4), (0, 2), (2, 2), (1, 4),
-    (0, 4), (2, 4),
+    (1, 5), (0, 4), (0, 4), (0, 0), (1, 0), (0, 1), (0, 0), (0, 5), (0, 5), (0, 3),
+    (1, 4), (1, 0), (0, 4), (1, 3), (0, 6), (0, 1), (0, 2), (1, 5), (0, 0), (1, 0),
+    (0, 3), (0, 5), (1, 5), (0, 4), (1, 3), (0, 1), (0, 2), (0, 6), (1, 4), (0, 0),
+    (0, 3), (1, 3), (1, 0), (0, 4), (1, 1), (0, 1), (1, 2), (1, 5), (0, 0), (0, 3),
+    (0, 2), (1, 6), (0, 5), (0, 6), (0, 4), (1, 4), (0, 3), (0, 1), (1, 3), (0, 2),
+    (1, 6), (1, 0), (1, 1), (0, 4), (0, 0), (1, 5), (1, 2), (0, 5), (0, 6), (0, 3),
+    (1, 4), (1, 1), (0, 2), (1, 3), (0, 0), (1, 2), (0, 1), (1, 0), (0, 6), (0, 4),
+    (1, 4), (0, 5), (0, 3), (1, 6), (1, 1), (1, 2), (0, 2), (1, 5), (1, 3), (0, 1),
+    (0, 4), (0, 5), (0, 6), (0, 0), (1, 2), (1, 6), (1, 1), (0, 3), (0, 2), (0, 0),
+    (2, 0), (0, 6), (1, 6), (0, 1), (1, 4), (2, 4), (0, 5), (0, 3), (2, 3), (0, 2),
+    (1, 2), (1, 1), (0, 1), (2, 1), (0, 5), (2, 5), (0, 6), (1, 6), (0, 2), (2, 2),
+    (0, 6), (2, 6),
 )
 MESH = pl.DeviceIdType.MESH
 COPIES = 264
@@ -60,7 +60,7 @@
     h_tin, h_tgr, h_eid, h_tid, h_bin, h_bout, h_eig, h_qin, h_qout,
     o_total, o_inf, o_task,
     tin, tgr, eid, tid, b_in, b_out, eig, qin, qout,
-    bt_in, bt_out, inv, total_bf,
+    bt_in, bt_out, inv, total_bf, chosen,
     pb, fb, ls, lx, lz, lw, cz, pq, fq, ly, le, li,
     s_hi, s_lo, part, ar_c, ar_p, ar_z,
     send_sem, recv_sem, load_sem,
@@ -356,14 +356,15 @@
             loads[6].wait()
             inv[...] = 1.0 / (eig[...] + DAMPING)
             make_scaled()
+            lane = lax.broadcasted_iota(jnp.int32, (QC, LANES), 1)
+            row = lax.broadcasted_iota(jnp.int32, (QC, LANES), 0)
+            chosen[...] = (row // RANK == lane).astype(jnp.bfloat16)
         else:
             influence_of(s)
         tick[0] += 1
         drain(tick[0] - 16)
 
-    lane = lax.broadcasted_iota(jnp.int32, (QC, LANES), 1)
-    row = lax.broadcasted_iota(jnp.int32, (QC, LANES), 0)
-    value = select_dot(part[...], (row // RANK == lane).astype(jnp.bfloat16))
+    value = select_dot(part[...], chosen[...])
 
     def reduce(value, slots, index, targets):
         slots[index] = value
@@ -410,6 +411,7 @@
         vm((IB, JB), bf16),
         vm((IB, JB), f32),
         vm((IB, JB), bf16),
+        vm((QC, LANES), bf16),
         vm((TOTAL * 4, LANES), f32),
         vm((TOTAL * 4, LANES), f32),
         vm((TOTAL * 2, LANES), f32),

time: 107 us -> 106 us (level)
  Pallas kernels: 107 us -> 105 us
    pallas_call x1, Pallas kernels: 105 us -> 103 us  [shards(): pl.pallas_call(kernel, out_shape=shapes, in_specs=[pl.BlockSpec(memory_sp...]
where the time goes in v4:
time: 106 us
  Pallas kernels  105 us (99%)
    pallas_call x1, Pallas kernels, shards(): pl.pallas_call(kernel, out_shape=shapes, in_specs=[pl.BlockSpec(memory_sp...  103 us

profile of v4, /device:TPU:1, one launch (start us, length us, event | category | flops | bytes accessed | tf_op | source)
XLA Modules:
  0.0 105.6 jit_solution(11622603494969415520)
XLA Ops:
  0.6 103.2 %influence.1 = (bf16[256,512]{1,0:T(8,128)(2,1)}, f32[4,48]{1,0:T(4,128)}, f32[4,16]{1,0:T(4,128)}) custom-call(bf16[256,256]{1,0:T(8,128)(2,1)} %h_tin.1, bf16[256,512]{1,0:T(8,128)(2,1)} %h_tgr.1, s32[1,256]{1,0:T(1,128)} %bitcast.2, s32[1,48]{1,0:T(1,128)} %bitcast.3, bf16[256,512]{1,0:T(8,128)(2,1)} %h_bin.1, bf16[512,256]{1,0:T(8,128)(2,1)} %h_bout.1, ...), custom_call_target="tpu_custom_call" | custom-call | tf_op jit(solution)/shard_map/influence/pallas_call | solution.py:442
  103.9 1.7 %finish.1 = (bf16[256,512]{1,0:T(8,128)(2,1)}, f32[4,48]{1,0:T(4,128)}, f32[4,16]{1,0:T(4,128)}) custom-call(bf16[256,512]{1,0:T(8,128)(2,1)} %get-tuple-element.6.refs_0_, f32[4,48]{1,0:T(4,128)} %get-tuple-element.7.refs_1_, f32[4,16]{1,0:T(4,128)} %get-tuple-element.8.refs_2_), custom_call_target="tpu_custom_call" | custom-call | tf_op jit(solution)/shard_map/finish/pallas_call | solution.py:453

commit v5 on v4

--- a/solution.py
+++ b/solution.py
@@ -38,7 +38,6 @@
 )
 MESH = pl.DeviceIdType.MESH
 COPIES = 264
-EARLY = 7
 
 
 def dot(a, b, contract=((1,), (0,))):
@@ -337,19 +336,21 @@
                 part[n:n + 1, at:at + many * LANES] = jnp.sum(weighted * out, axis=0, keepdims=True)
 
     part[...] = jnp.zeros_like(part)
-    begun = set()
     chains = [[basis_stage(s) for s in range(STAGES)], [query_stage(s) for s in range(STAGES)]]
-    for s in range(EARLY):
-        if s == 1:
-            loads[4].wait()
-            loads[5].wait()
+    next(chains[0][0])
+    next(chains[1][0])
+    pl.semaphore_wait(barrier, len(peers))
+    next(chains[0][0])
+    next(chains[1][0])
+    loads[4].wait()
+    loads[5].wait()
+    for s in range(1, STAGES):
         next(chains[0][s])
         next(chains[1][s])
-    pl.semaphore_wait(barrier, len(peers))
-    for kind, s in ORDER:
-        if kind < 2 and s >= EARLY and (kind, s) not in begun:
-            next(chains[kind][s])
-            begun.add((kind, s))
+    steps = list(ORDER)
+    steps.remove((0, 0))
+    steps.remove((1, 0))
+    for kind, s in steps:
         if kind < 2:
             next(chains[kind][s], None)
         elif s == 0:

time: 106 us -> 108 us (1.019)
  Pallas kernels: 105 us -> 107 us
    pallas_call x1, Pallas kernels: 103 us -> 105 us  [shards(): pl.pallas_call(kernel, out_shape=shapes, in_specs=[pl.BlockSpec(memory_sp...]
where the time goes in v5:
time: 108 us; the launch traced here: 107 us
  Pallas kernels  107 us (99%)
    pallas_call x1, Pallas kernels, shards(): pl.pallas_call(kernel, out_shape=shapes, in_specs=[pl.BlockSpec(memory_sp...  105 us

profile of v5, /device:TPU:1, one launch (start us, length us, event | category | flops | bytes accessed | tf_op | source)
XLA Modules:
  0.0 107.4 jit_solution(14996235735188811308)
XLA Ops:
  0.6 105.0 %influence.1 = (bf16[256,512]{1,0:T(8,128)(2,1)}, f32[4,48]{1,0:T(4,128)}, f32[4,16]{1,0:T(4,128)}) custom-call(bf16[256,256]{1,0:T(8,128)(2,1)} %h_tin.1, bf16[256,512]{1,0:T(8,128)(2,1)} %h_tgr.1, s32[1,256]{1,0:T(1,128)} %bitcast.2, s32[1,48]{1,0:T(1,128)} %bitcast.3, bf16[256,512]{1,0:T(8,128)(2,1)} %h_bin.1, bf16[512,256]{1,0:T(8,128)(2,1)} %h_bout.1, ...), custom_call_target="tpu_custom_call" | custom-call | tf_op jit(solution)/shard_map/influence/pallas_call | solution.py:443
  105.7 1.7 %finish.1 = (bf16[256,512]{1,0:T(8,128)(2,1)}, f32[4,48]{1,0:T(4,128)}, f32[4,16]{1,0:T(4,128)}) custom-call(bf16[256,512]{1,0:T(8,128)(2,1)} %get-tuple-element.6.refs_0_, f32[4,48]{1,0:T(4,128)} %get-tuple-element.7.refs_1_, f32[4,16]{1,0:T(4,128)} %get-tuple-element.8.refs_2_), custom_call_target="tpu_custom_call" | custom-call | tf_op jit(solution)/shard_map/finish/pallas_call | solution.py:454
